TPU v7x, 128 devices: a whole 4x4x4 slice. The times are simulated.
128 devices in a mesh: row: 16 (over y_hi, x, core), col: 8 (over y_lo, z).
Axes of the slice: x: 4, y: 4 (y_hi: 2, y_lo: 2; y = y_hi * 2 + y_lo), z: 4, core: 2. Of those that a mesh axis runs over, the one named last changes fastest.
Arguments:
- inputs: bfloat16 [1024, 12288], P('col', 'row'), may hold values from -6 to 6
- weight: bfloat16 [12288, 49152], P('row', 'col'), may hold values from -0.0546875 to 0.0546875
- cotangent: bfloat16 [1024, 49152], P('row', 'col'), may hold values from -6 to 6
Outputs:
- activated: bfloat16 [1024, 49152], P('row', 'col')
- grad_input: bfloat16 [1024, 12288], P('col', 'row')
- grad_weight: bfloat16 [12288, 49152], P('row', 'col')
All inputs are finite; a program needn't handle non-finite values.
Results may differ from a plain program's by a relative error of at most 0.022.
Values may be sent and summed in bfloat16 or wider, within the bound.
A program may use at most 128 MiB of HBM per device.

v0:
```python
import jax
import jax.numpy as jnp
from jax import lax
from jax.sharding import PartitionSpec as P

root_coef = 0.7978845608
cube_coef = 0.044715


def gelu_value(pre):
    inner = root_coef * (pre + cube_coef * pre * pre * pre)
    return 0.5 * pre * (1.0 + jnp.tanh(inner))


def gelu_slope(pre):
    tangent = jnp.tanh(root_coef * (pre + cube_coef * pre * pre * pre))
    return 0.5 * (1.0 + tangent) + 0.5 * pre * (1.0 - tangent * tangent) * root_coef * (
        1.0 + 3.0 * cube_coef * pre * pre
    )


def shards(inputs, weight, cotangent):
    gathered = lax.all_gather(inputs, "col", axis=0, tiled=True)
    piece = gathered
    pre = lax.psum_scatter(
        jnp.dot(piece, weight, preferred_element_type=jnp.float32).astype(jnp.bfloat16),
        "row",
        scatter_dimension=0,
        tiled=True,
    ).astype(jnp.float32)
    activated = gelu_value(pre).astype(jnp.bfloat16)
    grad_pre = (cotangent.astype(jnp.float32) * gelu_slope(pre)).astype(jnp.bfloat16)
    grad_all = lax.all_gather(grad_pre, "row", axis=0, tiled=True)
    piece = grad_all
    grad_input = lax.psum_scatter(
        lax.dot_general(
            piece, weight, (((1,), (1,)), ((), ())), preferred_element_type=jnp.float32
        ).astype(jnp.bfloat16),
        "col",
        scatter_dimension=0,
        tiled=True,
    )
    grad_weight = lax.dot_general(
        gathered, grad_all, (((0,), (0,)), ((), ())), preferred_element_type=jnp.float32
    ).astype(jnp.bfloat16)
    return (activated, grad_input, grad_weight)


def solution(mesh):
    placed = (P("col", "row"), P("row", "col"), P("row", "col"))
    return jax.shard_map(
        shards,
        mesh=mesh,
        in_specs=placed,
        out_specs=(P("row", "col"), P("col", "row"), P("row", "col")),
        check_vma=False,
    )
```

profile of v0, /device:TPU:1, one launch (start us, length us, event | category | flops | bytes accessed | tf_op | source)
XLA Modules:
  0.0 340.1 jit_solution(5342837406141239682)
XLA Ops:
  7.2 0.0 all-gather.3.cloned.1.call-start
  7.2 0.7 all-gather.3.cloned.1.call-update
  7.9 0.0 reduce-scatter.3.cloned.1.call-start
  7.9 39.5 %all-gather.3.cloned.1.call-done = bf16[1024,768]{1,0:T(8,128)(2,1)} async-done(((bf16[128,768]{1,0:T(8,128)(2,1)}), bf16[1024,768]{1,0:T(8,128)(2,1)}) %all-gather.3.cloned.1.call-update) | async-done | bytes 1572880 | tf_op jit(solution)/shard_map/all_gather | solution.py:23
  47.4 15.7 %convolution_convert_fusion = bf16[1024,6144]{1,0:T(8,128)(2,1)} fusion(bf16[1024,768]{1,0:T(8,128)(2,1)} %all-gather.3.cloned.1.call-done, bf16[768,6144]{1,0:T(8,128)(2,1)} %param.4), kind=kOutput, calls=%fused_computation | convolution fusion | flops 9669967872 | bytes 23592960 | tf_op jit(solution)/shard_map/dot_general | solution.py:26
  63.1 0.0 copy-start
  63.1 0.0 reduce-scatter.3.cloned.1.call-update
  63.1 0.0 all-gather.5.cloned.1.call-start
  63.2 127.0 %reduce-scatter.3.cloned.1.call-done = bf16[64,6144]{1,0:T(8,128)(2,1)} async-done(((bf16[1024,6144]{1,0:T(8,128)(2,1)}), bf16[64,6144]{1,0:T(8,128)(2,1)}) %reduce-scatter.3.cloned.1.call-update) | async-done | bytes 786448 | tf_op jit(solution)/shard_map/reduce_scatter | solution.py:25
  190.1 0.0 copy-done
  190.1 3.4 %fusion.8 = (bf16[64,6144]{1,0:T(8,128)(2,1)}, bf16[64,6144]{1,0:T(8,128)(2,1)}) fusion(bf16[64,6144]{1,0:T(8,128)(2,1)} %reduce-scatter.3.cloned.1.call-done, bf16[64,6144]{1,0:T(8,128)(2,1)S(1)} %copy-done), kind=kLoop, calls=%fused_computation.18 | loop fusion | flops 9043968 | bytes 3145728 | tf_op jit(solution)/shard_map/convert_element_type | solution.py:32
  193.6 0.0 all-gather.5.cloned.1.call-update
  193.6 0.2 reduce-scatter.5.cloned.1.call-start
  193.8 90.4 %all-gather.5.cloned.1.call-done = bf16[1024,6144]{1,0:T(8,128)(2,1)} async-done(((bf16[64,6144]{1,0:T(8,128)(2,1)}), bf16[1024,6144]{1,0:T(8,128)(2,1)}) %all-gather.5.cloned.1.call-update) | async-done | bytes 12582928 | tf_op jit(solution)/shard_map/all_gather | solution.py:33
  284.2 15.7 %convolution_convert_fusion.2 = bf16[1024,768]{1,0:T(8,128)(2,1)} fusion(bf16[1024,6144]{1,0:T(8,128)(2,1)} %all-gather.5.cloned.1.call-done, bf16[768,6144]{1,0:T(8,128)(2,1)} %param.4), kind=kOutput, calls=%fused_computation.12 | convolution fusion | flops 9664462848 | bytes 23592960 | tf_op jit(solution)/shard_map/dot_general | solution.py:36
  299.9 0.0 copy-start.1
  299.9 0.0 reduce-scatter.5.cloned.1.call-update
  299.9 1.4 copy-done.1
  301.3 17.3 %fusion = bf16[768,6144]{0,1:T(8,128)(2,1)} fusion(bf16[1024,6144]{1,0:T(8,128)(2,1)} %all-gather.5.cloned.1.call-done, bf16[1024,768]{1,0:T(8,128)(2,1)S(1)} %copy-done.1), kind=kOutput, calls=%fused_computation.2 | convolution fusion | flops 9668395008 | bytes 23592960 | tf_op jit(solution)/shard_map/dot_general | solution.py:43
  318.6 12.6 %copy.6 = bf16[768,6144]{1,0:T(8,128)(2,1)} copy(bf16[768,6144]{0,1:T(8,128)(2,1)} %fusion) | data formatting | bytes 18874368
  331.3 2.3 reduce-scatter.5.cloned.1.call-done
Async XLA Ops:
  7.2 40.2 %all-gather.3.cloned.1.call-start = ((), (), s32[]{:S(2)}) async-start(), calls=%async_computation.2 | async-start | bytes 1769472 | tf_op jit(solution)/shard_map/all_gather | solution.py:23
  7.9 182.2 %reduce-scatter.3.cloned.1.call-start = ((), (), s32[]{:S(2)}) async-start(), calls=%async_computation.3 | async-start | bytes 13369344 | tf_op jit(solution)/shard_map/reduce_scatter | solution.py:25
  63.1 127.1 %copy-start = (bf16[64,6144]{1,0:T(8,128)(2,1)S(1)}, bf16[64,6144]{1,0:T(8,128)(2,1)}, u32[]{:S(2)}) copy-start(bf16[64,6144]{1,0:T(8,128)(2,1)} %param.5) | copy-start | bytes 2359300
  63.1 221.1 %all-gather.5.cloned.1.call-start = ((), (), s32[]{:S(2)}) async-start(), calls=%async_computation.4 | async-start | bytes 13369344 | tf_op jit(solution)/shard_map/all_gather | solution.py:33
  193.6 140.0 %reduce-scatter.5.cloned.1.call-start = ((), (), s32[]{:S(2)}) async-start(), calls=%async_computation.5 | async-start | bytes 1769472 | tf_op jit(solution)/shard_map/reduce_scatter | solution.py:35
  299.9 1.4 copy-start.1
Sparse Core Ops, SparseCore 0:
  9.6 37.7 all-gather.2
  63.2 126.8 reduce-scatter.2
  193.7 90.4 all-gather.4
  300.1 33.4 reduce-scatter.4
where the time goes:
time: 345 us; the launch traced here: 340 us
  waiting for transfers between devices  260 us (75%)
  matrix products  48.7 us (14%)
  local copies, waits for them, and re-layouts  14 us (4%)
  between operations  13.8 us (4%)
    reduce_scatter x1, waiting for transfers between devices, shards(): lax.psum_scatter(jnp.dot(piece, weight, preferred_element_type=jnp.float3...  127 us
    all_gather x1, waiting for transfers between devices, shards(): grad_all = lax.all_gather(grad_pre, 'row', axis=0, tiled=True)  90.4 us
    all_gather x1, waiting for transfers between devices, shards(): gathered = lax.all_gather(inputs, 'col', axis=0, tiled=True)  39.5 us
    dot_general x1, matrix products, shards(): lax.dot_general(gathered, grad_all, (((0,), (0,)), ((), ())), preferred_e...  17.3 us
    dot_general x1, matrix products, shards(): lax.dot_general(piece, weight, (((1,), (1,)), ((), ())), preferred_elemen...  15.7 us
    dot_general x1, matrix products, shards(): jnp.dot(piece, weight, preferred_element_type=jnp.float32)  15.7 us
    unnamed x5, local copies, waits for them, and re-layouts  14 us
  transfers between devices with their start and end apart: 4, of which 4 were waited for; matrix products, arithmetic and copies ran while one was open for 9% of the time, Pallas kernels for 0%

commit v1 on v0

v1 whole, which is shorter than its diff:
```python
import jax
import jax.numpy as jnp
from jax import lax
from jax.experimental import pallas as pl
from jax.experimental.pallas import tpu as pltpu
from jax.sharding import PartitionSpec as P

MESH = pl.DeviceIdType.MESH
F32 = jnp.float32
BF16 = jnp.bfloat16

root_coef = 0.7978845608
cube_coef = 0.044715

CHUNKS = 4
ROWS = 16
WIDTH = 768
COLS = 6144
TILE = 512
A_COLS = 2560
B_COLS = COLS - A_COLS
A = slice(0, A_COLS)
B = slice(A_COLS, COLS)

NAMES = (
    ["xy", "cA", "cB", "sBy", "sAy", "gAy", "gBy", "gc", "iy"]
    + [f"{n}{d}" for n in ("xz", "xf", "sAx", "sBx", "gAx", "gBx", "gAf", "gBf", "iz") for d in (1, 2, 3)]
)
SLOT = {name: i for i, name in enumerate(NAMES)}


def kernel(
    x_ref, w_hbm, cot_ref,
    act_ref, gi_ref, g_hbm, x_out,
    w, xs, part, share, ra, ta, ray, rb, tb, rbx, grad, acc, gi, rz, ti, ry,
    send_sem, recv_sem, local_sem,
):
    row, col = lax.axis_index("row"), lax.axis_index("col")
    yhi, x, core = row // 8, (row // 2) % 4, row % 2
    ylo, z = col // 4, col % 4

    def device(yhi=yhi, x=x, core=core, ylo=ylo, z=z):
        return (yhi * 8 + x * 2 + core, ylo * 4 + z)

    y_peer = device(yhi=1 - yhi)
    core_peer = device(core=1 - core)
    ylo_peer = device(ylo=1 - ylo)
    x_at = {d: lax.rem(x + d, 4) for d in (1, 2, 3)}
    z_at = {d: lax.rem(z + d, 4) for d in (1, 2, 3)}
    x_peer = {d: device(x=x_at[d]) for d in (1, 2, 3)}
    z_peer = {d: device(z=z_at[d]) for d in (1, 2, 3)}
    peers = [y_peer, core_peer, ylo_peer, *x_peer.values(), *z_peer.values()]

    load_w = pltpu.make_async_copy(w_hbm, w, local_sem.at[0])
    load_w.start()

    barrier = pltpu.get_barrier_semaphore()
    for peer in peers:
        pl.semaphore_signal(barrier, inc=1, device_id=peer, device_id_type=MESH)
    pl.semaphore_wait(barrier, len(peers))

    copies = {}

    def send(k, name, src, dst, peer):
        copy = pltpu.make_async_remote_copy(
            src_ref=src, dst_ref=dst,
            send_sem=send_sem.at[k, SLOT[name]], recv_sem=recv_sem.at[k, SLOT[name]],
            device_id=peer, device_id_type=MESH,
        )
        copy.start()
        copies[k, name] = copy

    def arrived(k, *names):
        for name in names:
            copies[k, name].wait_recv()

    def three(name):
        return [f"{name}{d}" for d in (1, 2, 3)]

    def x_start(k):
        xs[k, :, col] = x_ref[:, k]
        send(k, "xy", x_ref.at[:, k], xs.at[k, :, col], ylo_peer)
        for d in (1, 2, 3):
            send(k, f"xz{d}", x_ref.at[:, k], xs.at[k, :, col], z_peer[d])

    def x_forward(k):
        arrived(k, "xy")
        other = (1 - ylo) * 4 + z
        for d in (1, 2, 3):
            send(k, f"xf{d}", xs.at[k, :, other], xs.at[k, :, other], z_peer[d])

    def tiles(first, last, body):
        @pl.loop(first, last)
        def _(j):
            body(pl.ds(pl.multiple_of(j * TILE, TILE), TILE))

    def product(k):
        arrived(k, *three("xz"), *three("xf"))
        if k >= 2:
            copies[k - 2, "cA"].wait_send()
            copies[k - 2, "cB"].wait_send()
        lhs = xs.at[k]

        def body(cols):
            out = jnp.dot(lhs[...].reshape(256, WIDTH), w[:, cols], preferred_element_type=F32)
            part[k % 2, :, :, :, cols] = out.astype(BF16).reshape(2, 8, ROWS, TILE)

        tiles(A_COLS // TILE, COLS // TILE, body)
        send(k, "cB", part.at[k % 2, 1 - core, :, :, B], share.at[k, :, :, B], core_peer)
        tiles(0, A_COLS // TILE, body)
        send(k, "cA", part.at[k % 2, 1 - core, :, :, A], share.at[k, :, :, A], core_peer)

    def reduce_first(k):
        def body(cols):
            mine = part[k % 2, core, :, :, cols].astype(F32)
            share[k, :, :, cols] = (mine + share[k, :, :, cols].astype(F32)).astype(BF16)

        arrived(k, "cB")
        tiles(A_COLS // TILE, COLS // TILE, body)
        send(k, "sBy", share.at[k, pl.ds((1 - yhi) * 4, 4), :, B], rb.at[k], y_peer)
        arrived(k, "cA")
        tiles(0, A_COLS // TILE, body)
        for d in (1, 2, 3):
            send(k, f"sAx{d}", share4(k).at[:, x_at[d], :, A], ra.at[k, d - 1], x_peer[d])

    def share4(k):
        return share.at[k].reshape(2, 4, ROWS, COLS)

    def reduce_second(k):
        arrived(k, "sBy")

        def body_b(j):
            cols = pl.ds(pl.multiple_of(A_COLS + j * TILE, TILE), TILE)
            here = pl.ds(pl.multiple_of(j * TILE, TILE), TILE)
            mine = share[k, pl.ds(yhi * 4, 4), :, cols].astype(F32)
            tb[k, :, :, here] = (mine + rb[k, :, :, here].astype(F32)).astype(BF16)

        pl.loop(0, B_COLS // TILE)(body_b)
        for d in (1, 2, 3):
            send(k, f"sBx{d}", tb.at[k, x_at[d]], rbx.at[k, d - 1], x_peer[d])
        arrived(k, *three("sAx"))

        def body_a(cols):
            for h in (0, 1):
                total = share[k, h * 4 + x, :, cols].astype(F32)
                for d in range(3):
                    total += ra[k, d, h, :, cols].astype(F32)
                ta[k, h, :, cols] = total.astype(BF16)

        tiles(0, A_COLS // TILE, body_a)
        send(k, "sAy", ta.at[k, 1 - yhi], ray.at[k], y_peer)

    def activate(k, pre, cols):
        tangent = jnp.tanh(root_coef * (pre + cube_coef * pre * pre * pre))
        act_ref[k, :, cols] = (0.5 * pre * (1.0 + tangent)).astype(BF16)
        slope = 0.5 * (1.0 + tangent) + 0.5 * pre * (1.0 - tangent * tangent) * root_coef * (
            1.0 + 3.0 * cube_coef * pre * pre
        )
        grad[k, core, row // 2, :, cols] = (cot_ref[k, :, cols].astype(F32) * slope).astype(BF16)

    def finish(k):
        arrived(k, "sAy")

        def body_a(cols):
            activate(k, ta[k, yhi, :, cols].astype(F32) + ray[k, :, cols].astype(F32), cols)

        tiles(0, A_COLS // TILE, body_a)
        mine = grad.at[k, core, row // 2]
        send(k, "gAy", mine.at[:, A], mine.at[:, A], y_peer)
        for d in (1, 2, 3):
            send(k, f"gAx{d}", mine.at[:, A], mine.at[:, A], x_peer[d])
        arrived(k, *three("sBx"))

        def body_b(j):
            cols = pl.ds(pl.multiple_of(A_COLS + j * TILE, TILE), TILE)
            here = pl.ds(pl.multiple_of(j * TILE, TILE), TILE)
            pre = tb[k, x, :, here].astype(F32)
            for d in range(3):
                pre += rbx[k, d, :, here].astype(F32)
            activate(k, pre, cols)

        pl.loop(0, B_COLS // TILE)(body_b)
        send(k, "gBy", mine.at[:, B], mine.at[:, B], y_peer)
        for d in (1, 2, 3):
            send(k, f"gBx{d}", mine.at[:, B], mine.at[:, B], x_peer[d])

    def gather_forward(k):
        arrived(k, "gAy")
        block = grad.at[k, core, (1 - yhi) * 4 + x, :, A]
        for d in (1, 2, 3):
            send(k, f"gAf{d}", block, block, x_peer[d])
        for d in (1, 3, 2):
            arrived(k, f"gBx{d}")
            block = grad.at[k, core, yhi * 4 + lax.rem(x + 4 - d, 4), :, B]
            send(k, f"gBf{d}", block, block, y_peer)

    def gather_core(k):
        arrived(k, "gBy", *three("gAx"), *three("gAf"), *three("gBf"))
        send(k, "gc", grad.at[k, core], grad.at[k, core], core_peer)

    stores = []

    def back(k):
        arrived(k, "gc")
        store = pltpu.make_async_copy(grad.at[k], g_hbm.at[k], local_sem.at[1 + k])
        store.start()
        stores.append(store)
        acc[...] = jnp.zeros_like(acc)

        def body(cols):
            acc[...] += lax.dot_general(
                grad[k, :, :, :, cols].reshape(256, TILE), w[:, cols],
                (((1,), (1,)), ((), ())), preferred_element_type=F32,
            )

        tiles(0, COLS // TILE, body)
        gi[k] = acc[...].astype(BF16).reshape(2, 2, 4, ROWS, WIDTH)
        for d in (1, 3, 2):
            send(k, f"iz{d}", gi.at[k, :, :, z_at[d]], rz.at[k, d - 1], z_peer[d])

    def back_second(k):
        arrived(k, *three("iz"))
        total = gi[k, :, :, z].astype(F32)
        for d in range(3):
            total += rz[k, d].astype(F32)
        ti[k] = total.astype(BF16)
        send(k, "iy", ti.at[k, :, 1 - ylo], ry.at[k], ylo_peer)

    def back_third(k):
        arrived(k, "iy")
        gi_ref[:, k] = (ti[k, :, ylo].astype(F32) + ry[k].astype(F32)).astype(BF16)

    for k in range(CHUNKS):
        x_start(k)
    x_forward(0)
    load_w.wait()
    product(0)
    x_forward(1)
    reduce_first(0)
    product(1)
    x_forward(2)
    reduce_second(0)
    reduce_first(1)
    finish(0)
    product(2)
    x_forward(3)
    reduce_second(1)
    reduce_first(2)
    gather_forward(0)
    finish(1)
    product(3)
    gather_core(0)
    reduce_second(2)
    reduce_first(3)
    gather_forward(1)
    back(0)
    finish(2)
    gather_core(1)
    reduce_second(3)
    gather_forward(2)
    back_second(0)
    back(1)
    finish(3)
    gather_core(2)
    gather_forward(3)
    back_third(0)
    back_second(1)
    back(2)
    gather_core(3)
    back_third(1)
    back_second(2)
    x_store = pltpu.make_async_copy(xs, x_out, local_sem.at[5])
    x_store.start()
    back(3)
    back_third(2)
    back_second(3)
    back_third(3)
    x_store.wait()
    for store in stores:
        store.wait()
    for (k, name), copy in copies.items():
        if not (name in ("cA", "cB") and k < 2):
            copy.wait_send()


def exchange(inputs, weight, cotangent):
    vmem = pl.BlockSpec(memory_space=pltpu.VMEM)
    hbm = pl.BlockSpec(memory_space=pl.ANY)
    n = len(NAMES)
    return pl.pallas_call(
        kernel,
        out_shape=(
            jax.ShapeDtypeStruct((CHUNKS, ROWS, COLS), BF16),
            jax.ShapeDtypeStruct((2, CHUNKS, ROWS, WIDTH), BF16),
            jax.ShapeDtypeStruct((CHUNKS, 2, 8, ROWS, COLS), BF16),
            jax.ShapeDtypeStruct((CHUNKS, 2, 8, ROWS, WIDTH), BF16),
        ),
        in_specs=[vmem, hbm, vmem],
        out_specs=(vmem, vmem, hbm, hbm),
        scratch_shapes=[
            pltpu.VMEM((WIDTH, COLS), BF16),
            pltpu.VMEM((CHUNKS, 2, 8, ROWS, WIDTH), BF16),
            pltpu.VMEM((2, 2, 8, ROWS, COLS), BF16),
            pltpu.VMEM((CHUNKS, 8, ROWS, COLS), BF16),
            pltpu.VMEM((CHUNKS, 3, 2, ROWS, A_COLS), BF16),
            pltpu.VMEM((CHUNKS, 2, ROWS, A_COLS), BF16),
            pltpu.VMEM((CHUNKS, ROWS, A_COLS), BF16),
            pltpu.VMEM((CHUNKS, 4, ROWS, B_COLS), BF16),
            pltpu.VMEM((CHUNKS, 4, ROWS, B_COLS), BF16),
            pltpu.VMEM((CHUNKS, 3, ROWS, B_COLS), BF16),
            pltpu.VMEM((CHUNKS, 2, 8, ROWS, COLS), BF16),
            pltpu.VMEM((256, WIDTH), F32),
            pltpu.VMEM((CHUNKS, 2, 2, 4, ROWS, WIDTH), BF16),
            pltpu.VMEM((CHUNKS, 3, 2, 2, ROWS, WIDTH), BF16),
            pltpu.VMEM((CHUNKS, 2, 2, ROWS, WIDTH), BF16),
            pltpu.VMEM((CHUNKS, 2, ROWS, WIDTH), BF16),
            pltpu.SemaphoreType.DMA((CHUNKS, n)),
            pltpu.SemaphoreType.DMA((CHUNKS, n)),
            pltpu.SemaphoreType.DMA((6,)),
        ],
        compiler_params=pltpu.CompilerParams(
            collective_id=0, has_side_effects=True, vmem_limit_bytes=60 * 2**20
        ),
        cost_estimate=pl.CostEstimate(flops=2 * 2 * 1024 * WIDTH * COLS, bytes_accessed=40 * 2**20, transcendentals=0),
        name="exchange",
    )(inputs.reshape(2, CHUNKS, ROWS, WIDTH), weight, cotangent.reshape(CHUNKS, ROWS, COLS))


def shards(inputs, weight, cotangent):
    activated, grad_input, grads, tokens = exchange(inputs, weight, cotangent)
    grad_weight = lax.dot_general(
        tokens.reshape(1024, WIDTH), grads.reshape(1024, COLS),
        (((0,), (0,)), ((), ())), preferred_element_type=F32,
    ).astype(BF16)
    return activated.reshape(64, COLS), grad_input.reshape(128, WIDTH), grad_weight


def solution(mesh):
    return jax.shard_map(
        shards,
        mesh=mesh,
        in_specs=(P("col", "row"), P("row", "col"), P("row", "col")),
        out_specs=(P("row", "col"), P("col", "row"), P("row", "col")),
        check_vma=False,
    )
```

time: 345 us -> 174 us (0.50)
  waiting for transfers between devices: 260 us -> 0 us
  Pallas kernels: 0 us -> 154 us
  matrix products: 48.7 us -> 15.8 us
  between operations: 13.8 us -> 0.66 us
  local copies, waits for them, and re-layouts: 14 us -> 1.56 us
    pallas_call x0 -> x1, Pallas kernels: none -> 154 us  [exchange(): pl.pallas_call(kernel, out_shape=(jax.ShapeDtypeStruct((CHUNKS, ROWS, COL...]
    all_gather x2 -> x0, waiting for transfers between devices: 130 us -> none  [the longest x1 90.4 us: shards(): grad_all = lax.all_gather(grad_pre, 'row', axis=0, tiled=True)]
    reduce_scatter x2 -> x0, waiting for transfers between devices: 129 us -> none  [the longest x1 127 us: shards(): lax.psum_scatter(jnp.dot(piece, weight, preferred_element_type=jnp.float3...]
    dot_general x3 -> x1, matrix products: 48.7 us -> 15.8 us  [shards(): lax.dot_general(tokens.reshape(1024, WIDTH), grads.reshape(1024, COLS), (...]
    unnamed x5 -> x6, local copies, waits for them, and re-layouts: 14 us -> 1.56 us
  transfers between devices with their start and end apart: 4 -> 0, of which waited for: 4 -> 0; matrix products, arithmetic and copies ran while one was open for 9% -> 0% of each run, Pallas kernels for 0% -> 0%
where the time goes in v1:
time: 174 us; the launch traced here: 172 us
  Pallas kernels  154 us (89%)
  matrix products  15.8 us (9%)
    pallas_call x1, Pallas kernels, exchange(): pl.pallas_call(kernel, out_shape=(jax.ShapeDtypeStruct((CHUNKS, ROWS, COL...  154 us
    dot_general x1, matrix products, shards(): lax.dot_general(tokens.reshape(1024, WIDTH), grads.reshape(1024, COLS), (...  15.8 us

profile of v1, /device:TPU:1, one launch (start us, length us, event | category | flops | bytes accessed | tf_op | source)
XLA Modules:
  0.0 172.4 jit_solution(3117719805460418619)
XLA Ops:
  0.6 154.4 %exchange.1 = (bf16[4,16,6144]{2,1,0:T(8,128)(2,1)}, bf16[2,4,16,768]{3,2,1,0:T(8,128)(2,1)}, bf16[4,2,8,16,6144]{4,3,2,1,0:T(8,128)(2,1)}, bf16[4,2,8,16,768]{4,3,2,1,0:T(8,128)(2,1)}) custom-call(bf16[2,4,16,768]{3,2,1,0:T(8,128)(2,1)} %bitcast.13, bf16[768,6144]{1,0:T(8,128)(2,1)} %w_hbm.1, bf16[4,16,6144]{2,1,0:T(8,128)(2,1)} %bitcast.12), custom_call_target="tpu_custom_call" | custom-call | flops 19327352832 | bytes 41943040 | tf_op jit(solution)/shard_map/exchange/pallas_call | solution.py:290
  155.0 0.0 copy-start
  155.0 0.0 copy-start.1
  155.1 15.8 %bitcast_convert_fusion = bf16[768,6144]{1,0:T(8,128)(2,1)} fusion(bf16[4,2,8,16,768]{4,3,2,1,0:T(8,128)(2,1)} %get-tuple-element.9, bf16[4,2,8,16,6144]{4,3,2,1,0:T(8,128)(2,1)} %get-tuple-element.10), kind=kOutput, calls=%fused_computation | convolution fusion | flops 9668395008 | bytes 23592960 | tf_op jit(solution)/shard_map/dot_general | solution.py:331
  170.8 0.0 copy-done
  170.8 0.9 copy.9
  171.7 0.0 copy-done.1
  171.7 0.7 copy.10
Async XLA Ops:
  155.0 15.8 %copy-start = (bf16[4,16,6144]{2,1,0:T(8,128)(2,1)S(1)}, bf16[4,16,6144]{2,1,0:T(8,128)(2,1)}, u32[]{:S(2)}) copy-start(bf16[4,16,6144]{2,1,0:T(8,128)(2,1)} %get-tuple-element.7) | copy-start | bytes 2359300
  155.0 16.7 %copy-start.1 = (bf16[2,4,16,768]{3,2,1,0:T(8,128)(2,1)S(1)}, bf16[2,4,16,768]{3,2,1,0:T(8,128)(2,1)}, u32[]{:S(2)}) copy-start(bf16[2,4,16,768]{3,2,1,0:T(8,128)(2,1)} %get-tuple-element.8) | copy-start | bytes 589828

commit v2 on v0

v2 whole, which is shorter than its diff:
```python
import jax
import jax.numpy as jnp
from jax import lax
from jax.experimental import pallas as pl
from jax.experimental.pallas import tpu as pltpu
from jax.sharding import PartitionSpec as P

MESH = pl.DeviceIdType.MESH
F32 = jnp.float32
BF16 = jnp.bfloat16

root_coef = 0.7978845608
cube_coef = 0.044715

CHUNKS = 4
ROWS = 16
WIDTH = 768
COLS = 6144
TILE = 512
A_COLS = 3584
B_COLS = COLS - A_COLS
A = slice(0, A_COLS)
B = slice(A_COLS, COLS)
A_HALF = (slice(0, 1536), slice(1536, A_COLS))
B_HALF = (slice(0, 1536), slice(1536, B_COLS))
A_WIDE = 2048
B_WIDE = 1536
GROUP = 1024
WAYS = (0, 1)
HOPS = (1, 2, 3)
SLOTS = 56


def width(cols):
    return cols.stop - cols.start


def in_b(cols):
    return slice(A_COLS + cols.start, A_COLS + cols.stop)


def kernel(
    x_ref, w_hbm, cot_ref,
    act_ref, gi_ref, gw_hbm, g_out, x_out,
    w, xs, xt, xt_last, part, share, ah, ra, ta, ay, rb, tb, bh, rbx, grad, acc, gi, rz, rd, ti, ry, stage,
    send_sem, recv_sem, local_sem,
):
    row, col = lax.axis_index("row"), lax.axis_index("col")
    yhi, x, core = row // 8, (row // 2) % 4, row % 2
    ylo, z = col // 4, col % 4
    me = row // 2

    def device(yhi=yhi, x=x, core=core, ylo=ylo, z=z):
        return (yhi * 8 + x * 2 + core, ylo * 4 + z)

    y_peer = device(yhi=1 - yhi)
    core_peer = device(core=1 - core)
    ylo_peer = device(ylo=1 - ylo)
    near = (lax.rem(x + 1, 4), lax.rem(x + 3, 4))
    far = lax.rem(x + 2, 4)
    x_peer = tuple(device(x=at) for at in near)
    z_at = {d: lax.rem(z + d, 4) for d in HOPS}
    z_peer = {d: device(z=z_at[d]) for d in HOPS}
    both_peer = {d: device(ylo=1 - ylo, z=z_at[d]) for d in HOPS}
    peers = [y_peer, core_peer, ylo_peer, *x_peer, *z_peer.values(), *both_peer.values()]

    load_w = pltpu.make_async_copy(w_hbm, w, local_sem.at[0])
    load_w.start()

    barrier = pltpu.get_barrier_semaphore()
    for peer in peers:
        pl.semaphore_signal(barrier, inc=1, device_id=peer, device_id_type=MESH)
    pl.semaphore_wait(barrier, len(peers))

    copies = {}
    slots = [0] * CHUNKS
    unsent = {}
    stores = []
    gw_stores = []

    def send(k, name, src, dst, peer):
        slot = slots[k]
        slots[k] += 1
        copy = pltpu.make_async_remote_copy(
            src_ref=src, dst_ref=dst, send_sem=send_sem.at[k, slot], recv_sem=recv_sem.at[k, slot],
            device_id=peer, device_id_type=MESH,
        )
        copy.start()
        copies[k, name] = unsent[k, name] = copy

    def sent(k, *names):
        for name in names:
            unsent.pop((k, name)).wait_send()

    def arrived(k, *names):
        for name in names:
            copies[k, name].wait_recv()

    def each(name, of):
        return [(name, d) for d in of]

    def tiles(first, last, body):
        @pl.loop(first // TILE, last // TILE)
        def _(j):
            body(pl.ds(pl.multiple_of(j * TILE, TILE), TILE))

    def rows4(k):
        return share.at[k].reshape(2, 4, ROWS, COLS)

    def x_start(k):
        xs[k, :, col] = x_ref[:, k]
        send(k, "xy", x_ref.at[:, k], xs.at[k, :, col], ylo_peer)
        for d in (1, 3, 2):
            send(k, ("xz", d), x_ref.at[:, k], xs.at[k, :, col], z_peer[d])
        if k == 0:
            for d in (1, 3, 2):
                send(k, ("xf", d), x_ref.at[:, k], xs.at[k, :, col], both_peer[d])

    def x_forward(k):
        arrived(k, "xy")
        block = xs.at[k, :, (1 - ylo) * 4 + z]
        for d in (1, 3, 2):
            send(k, ("xf", d), block, block, z_peer[d])

    waited = set()

    def prod_a(k, h):
        product(k, ("cA", h), A_HALF[h])

    def prod_b(k, h):
        product(k, ("cB", h), in_b(B_HALF[h]))

    def product(k, name, cols):
        if not waited:
            load_w.wait()
        if k not in waited:
            waited.add(k)
            arrived(k, *(["xy"] if k == 0 else []), *each("xz", HOPS), *each("xf", HOPS))
        if k >= 2:
            sent(k - 2, name)

        def body(tile):
            out = jnp.dot(xs[k].reshape(256, WIDTH), w[:, tile], preferred_element_type=F32)
            part[k % 2, :, :, :, tile] = out.astype(BF16).reshape(2, 8, ROWS, TILE)

        tiles(cols.start, cols.stop, body)
        send(k, name, part.at[k % 2, 1 - core, :, :, cols], share.at[k, :, :, cols], core_peer)

    def add_cores(k, name, cols):
        arrived(k, name)

        def body(tile):
            mine = part[k % 2, core, :, :, tile].astype(F32)
            share[k, :, :, tile] = (mine + share[k, :, :, tile].astype(F32)).astype(BF16)

        tiles(cols.start, cols.stop, body)

    def ra1(k, h):
        cols = A_HALF[h]
        add_cores(k, ("cA", h), cols)
        n = width(cols)
        send(k, ("ah", h), rows4(k).at[:, far, :, cols], ah.at[k, h, :, :, 0:n], x_peer[h])
        send(k, ("an", 1 - h), rows4(k).at[:, near[1 - h], :, cols], ra.at[k, 1 - h, :, :, cols], x_peer[1 - h])

    def ra2(k, h):
        cols = A_HALF[h]
        arrived(k, ("ah", h))
        for y in (0, 1):
            at = y * 4 + near[h]
            total = share[k, at, :, cols].astype(F32) + ah[k, h, y, :, 0 : width(cols)].astype(F32)
            share[k, at, :, cols] = total.astype(BF16)
        send(k, ("am", h), rows4(k).at[:, near[h], :, cols], ra.at[k, h, :, :, cols], x_peer[h])

    def ra3(k):
        arrived(k, *each("an", WAYS), *each("am", WAYS))

        def body(tile):
            for y in (0, 1):
                total = share[k, y * 4 + x, :, tile].astype(F32)
                total += ra[k, 0, y, :, tile].astype(F32) + ra[k, 1, y, :, tile].astype(F32)
                ta[k, y, :, tile] = total.astype(BF16)

        tiles(0, A_COLS, body)
        send(k, "ay", ta.at[k, 1 - yhi], ay.at[k], y_peer)

    def rb1(k, h):
        cols = B_HALF[h]
        add_cores(k, ("cB", h), in_b(cols))
        send(k, ("by", h), share.at[k, pl.ds((1 - yhi) * 4, 4), :, in_b(cols)], rb.at[k, :, :, cols], y_peer)

    def rb2(k, h):
        cols = B_HALF[h]
        arrived(k, ("by", h))
        for at in range(4):
            total = share[k, yhi * 4 + at, :, in_b(cols)].astype(F32) + rb[k, at, :, cols].astype(F32)
            tb[k, at, :, cols] = total.astype(BF16)
        send(k, ("bh", h), tb.at[k, far, :, cols], bh.at[k, h, :, 0 : width(cols)], x_peer[h])
        send(k, ("bn", 1 - h), tb.at[k, near[1 - h], :, cols], rbx.at[k, 1 - h, :, cols], x_peer[1 - h])

    def rb3(k, h):
        cols = B_HALF[h]
        arrived(k, ("bh", h))
        total = tb[k, near[h], :, cols].astype(F32) + bh[k, h, :, 0 : width(cols)].astype(F32)
        tb[k, near[h], :, cols] = total.astype(BF16)
        send(k, ("bm", h), tb.at[k, near[h], :, cols], rbx.at[k, h, :, cols], x_peer[h])

    def activate(k, pre, cols):
        tangent = jnp.tanh(root_coef * (pre + cube_coef * pre * pre * pre))
        act_ref[k, :, cols] = (0.5 * pre * (1.0 + tangent)).astype(BF16)
        slope = 0.5 * (1.0 + tangent) + 0.5 * pre * (1.0 - tangent * tangent) * root_coef * (
            1.0 + 3.0 * cube_coef * pre * pre
        )
        grad[k, core, me, :, cols] = (cot_ref[k, :, cols].astype(F32) * slope).astype(BF16)

    def block(k, y, at, cols):
        return grad.at[k, core, y * 4 + at, :, cols]

    def pass_on(k, name, ref, peer):
        send(k, name, ref, ref, peer)

    def fin_a(k):
        arrived(k, "ay")

        def body(tile):
            activate(k, ta[k, yhi, :, tile].astype(F32) + ay[k, :, tile].astype(F32), tile)

        tiles(0, A_COLS, body)
        mine = block(k, yhi, x, A)
        pass_on(k, "gAy", mine, y_peer)
        for h in WAYS:
            pass_on(k, ("gA", h), mine, x_peer[h])

    def fin_b(k):
        arrived(k, *each("bn", WAYS), *each("bm", WAYS))

        @pl.loop(0, B_COLS // TILE)
        def _(j):
            here = pl.ds(pl.multiple_of(j * TILE, TILE), TILE)
            pre = tb[k, x, :, here].astype(F32) + rbx[k, 0, :, here].astype(F32) + rbx[k, 1, :, here].astype(F32)
            activate(k, pre, pl.ds(pl.multiple_of(A_COLS + j * TILE, TILE), TILE))

        mine = block(k, yhi, x, B)
        for h in WAYS:
            pass_on(k, ("gB", h), mine, x_peer[h])
        pass_on(k, "gBy", mine, y_peer)

    def relay(k, name, y, halves):
        for h in WAYS:
            pass_on(k, (name, h), block(k, y, near[1 - h], halves[h]), x_peer[h])

    def ga1(k):
        arrived(k, *each("gA", WAYS))
        relay(k, "gAr", yhi, A_HALF)

    def gp1(k):
        arrived(k, "gAy")
        for h in WAYS:
            pass_on(k, ("gP", h), block(k, 1 - yhi, x, A), x_peer[h])

    def gp2(k):
        arrived(k, *each("gP", WAYS))
        relay(k, "gPr", 1 - yhi, A_HALF)

    def gb1(k):
        arrived(k, *each("gB", WAYS))
        relay(k, "gBr", yhi, [in_b(cols) for cols in B_HALF])
        for h in WAYS:
            pass_on(k, ("gBz", h), block(k, yhi, near[h], B), y_peer)

    def to_core(k, name, y, cols):
        pass_on(k, name, grad.at[k, core, pl.ds(y * 4, 4), :, cols], core_peer)

    def gb2(k):
        arrived(k, *each("gBr", WAYS))
        pass_on(k, "gBy2", block(k, yhi, far, B), y_peer)
        to_core(k, ("oB", 0), yhi, B)

    def ca1(k):
        arrived(k, *each("gAr", WAYS))
        to_core(k, ("oA", 0), yhi, A)

    def ca2(k):
        arrived(k, *each("gPr", WAYS))
        to_core(k, ("oA", 1), 1 - yhi, A)

    def cb2(k):
        arrived(k, "gBy", *each("gBz", WAYS), "gBy2")
        to_core(k, ("oB", 1), 1 - yhi, B)

    def multiply_back(k, first, last):
        def body(tile):
            acc[...] += lax.dot_general(
                grad[k, :, :, :, tile].reshape(256, TILE), w[:, tile],
                (((1,), (1,)), ((), ())), preferred_element_type=F32,
            )

        tiles(first, last, body)

    def gi_b(k):
        arrived(k, *each("oB", WAYS))
        acc[...] = jnp.zeros_like(acc)
        multiply_back(k, A_COLS, COLS)

    def gi_a(k):
        arrived(k, *each("oA", WAYS))
        if k == CHUNKS - 1:
            store = pltpu.make_async_copy(grad.at[k], g_out, local_sem.at[1])
            store.start()
            stores.append(store)
            xt_last[...] = xs[k].reshape(256, WIDTH).T
            store = pltpu.make_async_copy(xt_last, x_out, local_sem.at[8])
            store.start()
            stores.append(store)
        multiply_back(k, 0, A_COLS)
        gi[k] = acc[...].astype(BF16).reshape(2, 2, 4, ROWS, WIDTH)
        if k < CHUNKS - 1:
            for d in (1, 3, 2):
                send(k, ("iz", d), gi.at[k, :, :, z_at[d]], rz.at[k, d - 1], z_peer[d])
        else:
            for d in (2, 1, 3):
                send(k, ("iz", d), gi.at[k, :, ylo, z_at[d]], rd.at[d - 1], z_peer[d])
                send(k, ("id", d), gi.at[k, :, 1 - ylo, z_at[d]], rd.at[2 + d], both_peer[d])
            send(k, "iy", gi.at[k, :, 1 - ylo, z], rd.at[6], ylo_peer)

    def gi2(k):
        arrived(k, *each("iz", HOPS))
        total = gi[k, :, :, z].astype(F32)
        for d in range(3):
            total += rz[k, d].astype(F32)
        ti[k] = total.astype(BF16)
        send(k, "iy", ti.at[k, :, 1 - ylo], ry.at[k], ylo_peer)

    def gi3(k):
        arrived(k, "iy")
        if k < CHUNKS - 1:
            total = ti[k, :, ylo].astype(F32) + ry[k].astype(F32)
        else:
            arrived(k, *each("iz", HOPS), *each("id", HOPS))
            total = gi[k, :, ylo, z].astype(F32)
            for d in range(7):
                total += rd[d].astype(F32)
        gi_ref[:, k] = total.astype(BF16)

    def gw(g):
        slot = g % 2
        if g == 0:
            xt[...] = xs[0 : CHUNKS - 1].reshape(256 * (CHUNKS - 1), WIDTH).T
        if g >= 2:
            gw_stores[g - 2].wait()

        @pl.loop(0, GROUP // TILE)
        def _(j):
            cols = pl.ds(pl.multiple_of(g * GROUP + j * TILE, TILE), TILE)
            out = jnp.dot(
                xt[...], grad[0 : CHUNKS - 1, :, :, :, cols].reshape(256 * (CHUNKS - 1), TILE),
                preferred_element_type=F32,
            )
            stage[slot, :, pl.ds(pl.multiple_of(j * TILE, TILE), TILE)] = out.astype(BF16)

        store = pltpu.make_async_copy(
            stage.at[slot], gw_hbm.at[g], local_sem.at[2 + g]
        )
        store.start()
        gw_stores.append(store)

    x_start(0)
    prod_a(0, 0)
    x_start(1)
    prod_a(0, 1)
    prod_b(0, 0)
    x_forward(1)
    ra1(0, 0)
    prod_b(0, 1)
    x_start(2)
    ra1(0, 1)
    rb1(0, 0)
    rb1(0, 1)
    prod_a(1, 0)
    x_forward(2)
    ra2(0, 0)
    prod_a(1, 1)
    ra2(0, 1)
    x_start(3)
    prod_b(1, 0)
    ra1(1, 0)
    prod_b(1, 1)
    ra1(1, 1)
    prod_a(2, 0)
    rb2(0, 1)
    rb2(0, 0)
    x_forward(3)
    ra3(0)
    rb1(1, 1)
    rb1(1, 0)
    ra2(1, 0)
    prod_a(2, 1)
    ra1(2, 0)
    rb3(0, 1)
    prod_b(2, 0)
    rb3(0, 0)
    prod_b(2, 1)
    ra2(1, 1)
    ra1(2, 1)
    prod_a(3, 0)
    fin_a(0)
    rb1(2, 0)
    rb1(2, 1)
    rb2(1, 1)
    fin_b(0)
    prod_a(3, 1)
    ra1(3, 0)
    ra2(2, 0)
    prod_b(3, 0)
    rb2(1, 0)
    prod_b(3, 1)
    ra1(3, 1)
    rb3(1, 1)
    ra3(1)
    rb1(3, 0)
    rb1(3, 1)
    ra2(2, 1)
    gp1(0)
    gb1(0)
    rb3(1, 0)
    ga1(0)
    rb2(2, 1)
    ra2(3, 0)
    rb3(2, 1)
    gb2(0)
    fin_b(1)
    rb2(2, 0)
    ca1(0)
    fin_a(1)
    ra2(3, 1)
    gp2(0)
    ra3(2)
    rb2(3, 1)
    rb3(2, 0)
    cb2(0)
    rb3(3, 1)
    gb1(1)
    rb2(3, 0)
    fin_b(2)
    ca2(0)
    gp1(1)
    gi_b(0)
    ga1(1)
    fin_a(2)
    gi_a(0)
    rb3(3, 0)
    gb2(1)
    ra3(3)
    gb1(2)
    ca1(1)
    fin_b(3)
    gp1(2)
    gp2(1)
    gi2(0)
    ga1(2)
    gb2(2)
    cb2(1)
    gi_b(1)
    fin_a(3)
    ca2(1)
    gb1(3)
    ca1(2)
    gi3(0)
    gp2(2)
    cb2(2)
    gi_a(1)
    gb2(3)
    ga1(3)
    ca2(2)
    gi_b(2)
    gp1(3)
    ca1(3)
    cb2(3)
    gi_a(2)
    gi2(1)
    gp2(3)
    gw(0)
    gi_b(3)
    ca2(3)
    gi3(1)
    gw(1)
    gi2(2)
    gw(2)
    gi_a(3)
    gi3(2)
    gw(3)
    gw(4)
    gw(5)
    gi3(3)

    for store in stores + gw_stores[-2:]:
        store.wait()
    for copy in unsent.values():
        copy.wait_send()


def exchange(inputs, weight, cotangent):
    vmem = pl.BlockSpec(memory_space=pltpu.VMEM)
    hbm = pl.BlockSpec(memory_space=pl.ANY)
    return pl.pallas_call(
        kernel,
        out_shape=(
            jax.ShapeDtypeStruct((CHUNKS, ROWS, COLS), BF16),
            jax.ShapeDtypeStruct((2, CHUNKS, ROWS, WIDTH), BF16),
            jax.ShapeDtypeStruct((COLS // GROUP, WIDTH, GROUP), BF16),
            jax.ShapeDtypeStruct((2, 8, ROWS, COLS), BF16),
            jax.ShapeDtypeStruct((WIDTH, 256), BF16),
        ),
        in_specs=[vmem, hbm, vmem],
        out_specs=(vmem, vmem, hbm, hbm, hbm),
        scratch_shapes=[
            pltpu.VMEM((WIDTH, COLS), BF16),
            pltpu.VMEM((CHUNKS, 2, 8, ROWS, WIDTH), BF16),
            pltpu.VMEM((WIDTH, 256 * (CHUNKS - 1)), BF16),
            pltpu.VMEM((WIDTH, 256), BF16),
            pltpu.VMEM((2, 2, 8, ROWS, COLS), BF16),
            pltpu.VMEM((CHUNKS, 8, ROWS, COLS), BF16),
            pltpu.VMEM((CHUNKS, 2, 2, ROWS, A_WIDE), BF16),
            pltpu.VMEM((CHUNKS, 2, 2, ROWS, A_COLS), BF16),
            pltpu.VMEM((CHUNKS, 2, ROWS, A_COLS), BF16),
            pltpu.VMEM((CHUNKS, ROWS, A_COLS), BF16),
            pltpu.VMEM((CHUNKS, 4, ROWS, B_COLS), BF16),
            pltpu.VMEM((CHUNKS, 4, ROWS, B_COLS), BF16),
            pltpu.VMEM((CHUNKS, 2, ROWS, B_WIDE), BF16),
            pltpu.VMEM((CHUNKS, 2, ROWS, B_COLS), BF16),
            pltpu.VMEM((CHUNKS, 2, 8, ROWS, COLS), BF16),
            pltpu.VMEM((256, WIDTH), F32),
            pltpu.VMEM((CHUNKS, 2, 2, 4, ROWS, WIDTH), BF16),
            pltpu.VMEM((CHUNKS - 1, 3, 2, 2, ROWS, WIDTH), BF16),
            pltpu.VMEM((7, 2, ROWS, WIDTH), BF16),
            pltpu.VMEM((CHUNKS - 1, 2, 2, ROWS, WIDTH), BF16),
            pltpu.VMEM((CHUNKS - 1, 2, ROWS, WIDTH), BF16),
            pltpu.VMEM((2, WIDTH, GROUP), BF16),
            pltpu.SemaphoreType.DMA((CHUNKS, SLOTS)),
            pltpu.SemaphoreType.DMA((CHUNKS, SLOTS)),
            pltpu.SemaphoreType.DMA((9,)),
        ],
        compiler_params=pltpu.CompilerParams(
            collective_id=0, has_side_effects=True, vmem_limit_bytes=61 * 2**20
        ),
        cost_estimate=pl.CostEstimate(flops=5 * 1024 * WIDTH * COLS, bytes_accessed=24 * 2**20, transcendentals=0),
        name="exchange",
    )(inputs.reshape(2, CHUNKS, ROWS, WIDTH), weight, cotangent.reshape(CHUNKS, ROWS, COLS))


def last_tokens(sum_hbm, x_hbm, g_hbm, o_hbm, total, x_t, grads, sem, out_sem):
    groups = COLS // GROUP
    tokens = pltpu.make_async_copy(x_hbm, x_t, sem.at[0])
    tokens.start()
    loads = []
    for g in range(groups):
        cols = slice(g * GROUP, (g + 1) * GROUP)
        pair = (
            pltpu.make_async_copy(g_hbm.at[:, :, :, cols], grads.at[:, :, :, cols], sem.at[1 + g]),
            pltpu.make_async_copy(sum_hbm.at[g], total.at[g], sem.at[1 + groups + g]),
        )
        for load in pair:
            load.start()
        loads.append(pair)
    tokens.wait()
    stores = []
    for g in range(groups):
        for load in loads[g]:
            load.wait()

        @pl.loop(0, GROUP // TILE)
        def _(j):
            here = pl.ds(pl.multiple_of(j * TILE, TILE), TILE)
            cols = pl.ds(pl.multiple_of(g * GROUP + j * TILE, TILE), TILE)
            more = jnp.dot(
                x_t[...], grads[:, :, :, cols].reshape(256, TILE), preferred_element_type=F32
            )
            total[g, :, here] = (total[g, :, here].astype(F32) + more).astype(BF16)

        store = pltpu.make_async_copy(total.at[g], o_hbm.at[:, g * GROUP : (g + 1) * GROUP], out_sem.at[g])
        store.start()
        stores.append(store)
    for store in stores:
        store.wait()


def add_last(partial, tokens, grads):
    hbm = pl.BlockSpec(memory_space=pl.ANY)
    groups = COLS // GROUP
    return pl.pallas_call(
        last_tokens,
        out_shape=jax.ShapeDtypeStruct((WIDTH, COLS), BF16),
        in_specs=[hbm, hbm, hbm],
        out_specs=hbm,
        scratch_shapes=[
            pltpu.VMEM((groups, WIDTH, GROUP), BF16),
            pltpu.VMEM((WIDTH, 256), BF16),
            pltpu.VMEM((2, 8, ROWS, COLS), BF16),
            pltpu.SemaphoreType.DMA((1 + 2 * groups,)),
            pltpu.SemaphoreType.DMA((groups,)),
        ],
        compiler_params=pltpu.CompilerParams(vmem_limit_bytes=60 * 2**20),
        cost_estimate=pl.CostEstimate(flops=2 * 256 * WIDTH * COLS, bytes_accessed=24 * 2**20, transcendentals=0),
        name="add_last",
    )(partial, tokens, grads)


def shards(inputs, weight, cotangent):
    activated, grad_input, partial, grads, tokens = exchange(inputs, weight, cotangent)
    grad_weight = add_last(partial, tokens, grads)
    return activated.reshape(64, COLS), grad_input.reshape(128, WIDTH), grad_weight


def solution(mesh):
    return jax.shard_map(
        shards,
        mesh=mesh,
        in_specs=(P("col", "row"), P("row", "col"), P("row", "col")),
        out_specs=(P("row", "col"), P("col", "row"), P("row", "col")),
        check_vma=False,
    )
```

time: 345 us -> 142 us (0.41); the launches traced: 340 us -> 141 us
  waiting for transfers between devices: 260 us -> 0 us
  Pallas kernels: 0 us -> 139 us
  matrix products: 48.7 us -> 0 us
  between operations: 13.8 us -> 0.67 us
  local copies, waits for them, and re-layouts: 14 us -> 1.57 us
    pallas_call x0 -> x2, Pallas kernels: none -> 139 us  [the longest x1 130 us: exchange(): pl.pallas_call(kernel, out_shape=(jax.ShapeDtypeStruct((CHUNKS, ROWS, COL...]
    all_gather x2 -> x0, waiting for transfers between devices: 130 us -> none  [the longest x1 90.4 us: shards(): grad_all = lax.all_gather(grad_pre, 'row', axis=0, tiled=True)]
    reduce_scatter x2 -> x0, waiting for transfers between devices: 129 us -> none  [the longest x1 127 us: shards(): lax.psum_scatter(jnp.dot(piece, weight, preferred_element_type=jnp.float3...]
    dot_general x3 -> x0, matrix products: 48.7 us -> none  [the longest x1 17.3 us: shards(): lax.dot_general(gathered, grad_all, (((0,), (0,)), ((), ())), preferred_e...]
    unnamed x5 -> x6, local copies, waits for them, and re-layouts: 14 us -> 1.57 us
  transfers between devices with their start and end apart: 4 -> 0, of which waited for: 4 -> 0; matrix products, arithmetic and copies ran while one was open for 9% -> 0% of each run, Pallas kernels for 0% -> 0%
where the time goes in v2:
time: 142 us; the launch traced here: 141 us
  Pallas kernels  139 us (98%)
  local copies, waits for them, and re-layouts  1.57 us (1%)
    pallas_call x1, Pallas kernels, exchange(): pl.pallas_call(kernel, out_shape=(jax.ShapeDtypeStruct((CHUNKS, ROWS, COL...  130 us
    pallas_call x1, Pallas kernels, add_last(): pl.pallas_call(last_tokens, out_shape=jax.ShapeDtypeStruct((WIDTH, COLS),...  9.11 us

profile of v2, /device:TPU:1, one launch (start us, length us, event | category | flops | bytes accessed | tf_op | source)
XLA Modules:
  0.0 141.3 jit_solution(12485394943134597285)
XLA Ops:
  0.6 130.0 %exchange.1 = (bf16[4,16,6144]{2,1,0:T(8,128)(2,1)}, bf16[2,4,16,768]{3,2,1,0:T(8,128)(2,1)}, bf16[6,768,1024]{2,1,0:T(8,128)(2,1)}, bf16[2,8,16,6144]{3,2,1,0:T(8,128)(2,1)}, bf16[768,256]{1,0:T(8,128)(2,1)}) custom-call(bf16[2,4,16,768]{3,2,1,0:T(8,128)(2,1)} %bitcast.7, bf16[768,6144]{1,0:T(8,128)(2,1)} %w_hbm.1, bf16[4,16,6144]{2,1,0:T(8,128)(2,1)} %bitcast.6), custom_call_target="tpu_custom_call" | custom-call | flops 24159191040 | bytes 25165824 | tf_op jit(solution)/shard_map/exchange/pallas_call | solution.py:504
  130.6 0.0 copy-start
  130.6 0.0 copy-start.1
  130.7 9.1 %add_last.1 = bf16[768,6144]{1,0:T(8,128)(2,1)} custom-call(bf16[6,768,1024]{2,1,0:T(8,128)(2,1)} %get-tuple-element.10.sum_hbm, bf16[768,256]{1,0:T(8,128)(2,1)} %get-tuple-element.11.x_hbm, bf16[2,8,16,6144]{3,2,1,0:T(8,128)(2,1)} %get-tuple-element.12.g_hbm), custom_call_target="tpu_custom_call" | custom-call | flops 2415919104 | bytes 25165824 | tf_op jit(solution)/shard_map/add_last/pallas_call | solution.py:589
  139.8 0.0 copy-done
  139.8 0.9 copy.8
  140.7 0.0 copy-done.1
  140.7 0.7 copy.9
Async XLA Ops:
  130.6 9.1 %copy-start = (bf16[4,16,6144]{2,1,0:T(8,128)(2,1)S(1)}, bf16[4,16,6144]{2,1,0:T(8,128)(2,1)}, u32[]{:S(2)}) copy-start(bf16[4,16,6144]{2,1,0:T(8,128)(2,1)} %get-tuple-element.8) | copy-start | bytes 2359300
  130.6 10.0 %copy-start.1 = (bf16[2,4,16,768]{3,2,1,0:T(8,128)(2,1)S(1)}, bf16[2,4,16,768]{3,2,1,0:T(8,128)(2,1)}, u32[]{:S(2)}) copy-start(bf16[2,4,16,768]{3,2,1,0:T(8,128)(2,1)} %get-tuple-element.9) | copy-start | bytes 589828

commit v3 on v2

--- a/solution.py
+++ b/solution.py
@@ -13,6 +13,7 @@
 cube_coef = 0.044715
 
 CHUNKS = 4
+LAST = CHUNKS - 1
 ROWS = 16
 WIDTH = 768
 COLS = 6144
@@ -28,7 +29,7 @@
 GROUP = 1024
 WAYS = (0, 1)
 HOPS = (1, 2, 3)
-SLOTS = 56
+SLOTS = 224
 
 
 def width(cols):
@@ -73,16 +74,14 @@
     pl.semaphore_wait(barrier, len(peers))
 
     copies = {}
-    slots = [0] * CHUNKS
     unsent = {}
     stores = []
     gw_stores = []
 
     def send(k, name, src, dst, peer):
-        slot = slots[k]
-        slots[k] += 1
+        slot = len(copies)
         copy = pltpu.make_async_remote_copy(
-            src_ref=src, dst_ref=dst, send_sem=send_sem.at[k, slot], recv_sem=recv_sem.at[k, slot],
+            src_ref=src, dst_ref=dst, send_sem=send_sem.at[slot], recv_sem=recv_sem.at[slot],
             device_id=peer, device_id_type=MESH,
         )
         copy.start()
@@ -256,10 +255,15 @@
         arrived(k, "gAy")
         for h in WAYS:
             pass_on(k, ("gP", h), block(k, 1 - yhi, x, A), x_peer[h])
+        if k == LAST:
+            pass_on(k, ("oA", 1), block(k, 1 - yhi, x, A), core_peer)
 
     def gp2(k):
         arrived(k, *each("gP", WAYS))
         relay(k, "gPr", 1 - yhi, A_HALF)
+        if k == LAST:
+            for h in WAYS:
+                pass_on(k, ("oA", 2 + h), block(k, 1 - yhi, near[h], A), core_peer)
 
     def gb1(k):
         arrived(k, *each("gB", WAYS))
@@ -281,46 +285,61 @@
 
     def ca2(k):
         arrived(k, *each("gPr", WAYS))
-        to_core(k, ("oA", 1), 1 - yhi, A)
+        if k == LAST:
+            pass_on(k, ("oA", 4), block(k, 1 - yhi, far, A), core_peer)
+        else:
+            to_core(k, ("oA", 1), 1 - yhi, A)
 
     def cb2(k):
         arrived(k, "gBy", *each("gBz", WAYS), "gBy2")
         to_core(k, ("oB", 1), 1 - yhi, B)
 
-    def multiply_back(k, first, last):
-        def body(tile):
-            acc[...] += lax.dot_general(
-                grad[k, :, :, :, tile].reshape(256, TILE), w[:, tile],
+    def multiply_back(k, first, last, cols):
+        def body(n):
+            at = pl.ds(pl.multiple_of(n * 256, 256), 256)
+            out = lax.dot_general(
+                grad[k, :, :, :, cols].reshape(256, width(cols)), w[at, cols],
                 (((1,), (1,)), ((), ())), preferred_element_type=F32,
             )
-
-        tiles(first, last, body)
+            if cols == B:
+                acc[k % 2, :, at] = out
+            else:
+                out += acc[k % 2, :, at]
+                gi[k, :, :, :, :, at] = out.astype(BF16).reshape(2, 2, 4, ROWS, 256)
+
+        pl.loop(first, last)(body)
 
     def gi_b(k):
         arrived(k, *each("oB", WAYS))
-        acc[...] = jnp.zeros_like(acc)
-        multiply_back(k, A_COLS, COLS)
+        multiply_back(k, 0, WIDTH // 256, B)
 
     def gi_a(k):
-        arrived(k, *each("oA", WAYS))
-        if k == CHUNKS - 1:
+        arrived(k, *each("oA", WAYS if k < LAST else range(5)))
+        if k < LAST:
+            multiply_back(k, 0, WIDTH // 256, A)
+            for d in (1, 3, 2):
+                send(k, ("iz", d), gi.at[k, :, :, z_at[d]], rz.at[k, d - 1], z_peer[d])
+        else:
             store = pltpu.make_async_copy(grad.at[k], g_out, local_sem.at[1])
             store.start()
             stores.append(store)
-            xt_last[...] = xs[k].reshape(256, WIDTH).T
-            store = pltpu.make_async_copy(xt_last, x_out, local_sem.at[8])
-            store.start()
-            stores.append(store)
-        multiply_back(k, 0, A_COLS)
-        gi[k] = acc[...].astype(BF16).reshape(2, 2, 4, ROWS, WIDTH)
-        if k < CHUNKS - 1:
-            for d in (1, 3, 2):
-                send(k, ("iz", d), gi.at[k, :, :, z_at[d]], rz.at[k, d - 1], z_peer[d])
-        else:
-            for d in (2, 1, 3):
-                send(k, ("iz", d), gi.at[k, :, ylo, z_at[d]], rd.at[d - 1], z_peer[d])
-                send(k, ("id", d), gi.at[k, :, 1 - ylo, z_at[d]], rd.at[2 + d], both_peer[d])
-            send(k, "iy", gi.at[k, :, 1 - ylo, z], rd.at[6], ylo_peer)
+            multiply_back(k, 0, 1, A)
+            last_out(0, slice(0, 256))
+
+    def gi_c(k):
+        multiply_back(k, 1, WIDTH // 256, A)
+        last_out(1, slice(256, WIDTH))
+        xt_last[...] = xs[k].reshape(256, WIDTH).T
+        store = pltpu.make_async_copy(xt_last, x_out, local_sem.at[8])
+        store.start()
+        stores.append(store)
+
+    def last_out(s, cols):
+        k = LAST
+        for d in (2, 1, 3):
+            send(k, ("iz", d, s), gi.at[k, :, ylo, z_at[d], :, cols], rd.at[d - 1, :, :, cols], z_peer[d])
+            send(k, ("id", d, s), gi.at[k, :, 1 - ylo, z_at[d], :, cols], rd.at[2 + d, :, :, cols], both_peer[d])
+        send(k, ("iy", s), gi.at[k, :, 1 - ylo, z, :, cols], rd.at[6, :, :, cols], ylo_peer)
 
     def gi2(k):
         arrived(k, *each("iz", HOPS))
@@ -331,11 +350,12 @@
         send(k, "iy", ti.at[k, :, 1 - ylo], ry.at[k], ylo_peer)
 
     def gi3(k):
-        arrived(k, "iy")
-        if k < CHUNKS - 1:
+        if k < LAST:
+            arrived(k, "iy")
             total = ti[k, :, ylo].astype(F32) + ry[k].astype(F32)
         else:
-            arrived(k, *each("iz", HOPS), *each("id", HOPS))
+            for s in WAYS:
+                arrived(k, ("iy", s), *[(n, d, s) for n in ("iz", "id") for d in HOPS])
             total = gi[k, :, ylo, z].astype(F32)
             for d in range(7):
                 total += rd[d].astype(F32)
@@ -364,133 +384,134 @@
         gw_stores.append(store)
 
     x_start(0)
+    x_start(1)
+    prod_b(0, 1)
     prod_a(0, 0)
-    x_start(1)
-    prod_a(0, 1)
     prod_b(0, 0)
     x_forward(1)
+    rb1(0, 1)
+    prod_a(0, 1)
     ra1(0, 0)
-    prod_b(0, 1)
     x_start(2)
+    rb1(0, 0)
+    prod_a(1, 0)
     ra1(0, 1)
-    rb1(0, 0)
-    rb1(0, 1)
-    prod_a(1, 0)
+    prod_b(1, 1)
+    rb2(0, 1)
+    ra2(0, 0)
     x_forward(2)
-    ra2(0, 0)
-    prod_a(1, 1)
-    ra2(0, 1)
-    x_start(3)
     prod_b(1, 0)
     ra1(1, 0)
-    prod_b(1, 1)
+    prod_a(1, 1)
+    rb3(0, 1)
+    rb2(0, 0)
+    rb1(1, 1)
+    x_start(3)
+    rb1(1, 0)
+    ra2(0, 1)
+    prod_b(2, 1)
+    prod_b(2, 0)
+    prod_a(2, 0)
+    rb1(2, 1)
     ra1(1, 1)
-    prod_a(2, 0)
-    rb2(0, 1)
-    rb2(0, 0)
+    prod_a(2, 1)
+    rb1(2, 0)
+    ra2(1, 0)
     x_forward(3)
+    ra1(2, 0)
     ra3(0)
-    rb1(1, 1)
-    rb1(1, 0)
-    ra2(1, 0)
-    prod_a(2, 1)
-    ra1(2, 0)
-    rb3(0, 1)
-    prod_b(2, 0)
     rb3(0, 0)
-    prod_b(2, 1)
+    ra1(2, 1)
+    rb2(1, 1)
     ra2(1, 1)
-    ra1(2, 1)
     prod_a(3, 0)
-    fin_a(0)
-    rb1(2, 0)
-    rb1(2, 1)
-    rb2(1, 1)
+    prod_b(3, 1)
+    prod_b(3, 0)
+    rb3(1, 1)
     fin_b(0)
     prod_a(3, 1)
+    rb1(3, 1)
     ra1(3, 0)
+    rb1(3, 0)
+    rb2(2, 1)
+    rb2(1, 0)
     ra2(2, 0)
-    prod_b(3, 0)
-    rb2(1, 0)
-    prod_b(3, 1)
+    fin_a(0)
     ra1(3, 1)
-    rb3(1, 1)
+    ra2(2, 1)
     ra3(1)
-    rb1(3, 0)
-    rb1(3, 1)
-    ra2(2, 1)
-    gp1(0)
+    rb3(2, 1)
     gb1(0)
     rb3(1, 0)
-    ga1(0)
-    rb2(2, 1)
+    rb2(2, 0)
     ra2(3, 0)
-    rb3(2, 1)
+    rb2(3, 1)
     gb2(0)
     fin_b(1)
-    rb2(2, 0)
+    gp1(0)
+    rb3(2, 0)
+    ga1(0)
+    ra2(3, 1)
+    ra3(2)
+    rb3(3, 1)
+    fin_a(1)
+    rb2(3, 0)
+    cb2(0)
+    fin_b(2)
     ca1(0)
-    fin_a(1)
-    ra2(3, 1)
+    gb1(1)
+    gi_b(0)
+    gp1(1)
+    fin_a(2)
+    rb3(3, 0)
     gp2(0)
-    ra3(2)
-    rb2(3, 1)
-    rb3(2, 0)
-    cb2(0)
-    rb3(3, 1)
-    gb1(1)
-    rb2(3, 0)
-    fin_b(2)
-    ca2(0)
-    gp1(1)
-    gi_b(0)
+    gb2(1)
     ga1(1)
-    fin_a(2)
-    gi_a(0)
-    rb3(3, 0)
-    gb2(1)
     ra3(3)
     gb1(2)
+    gp1(2)
+    fin_b(3)
+    cb2(1)
+    ca2(0)
+    gi_b(1)
+    gb2(2)
+    ga1(2)
+    gp2(1)
     ca1(1)
-    fin_b(3)
-    gp1(2)
-    gp2(1)
+    gi_a(0)
+    gb1(3)
+    gp2(2)
+    fin_a(3)
+    cb2(2)
+    ca1(2)
+    ca2(1)
+    gi_b(2)
+    gb2(3)
+    ca2(2)
     gi2(0)
-    ga1(2)
-    gb2(2)
-    cb2(1)
-    gi_b(1)
-    fin_a(3)
-    ca2(1)
-    gb1(3)
-    ca1(2)
+    ga1(3)
+    gi_a(1)
+    gp1(3)
+    gi_a(2)
+    cb2(3)
+    ca1(3)
     gi3(0)
-    gp2(2)
-    cb2(2)
-    gi_a(1)
-    gb2(3)
-    ga1(3)
-    ca2(2)
-    gi_b(2)
-    gp1(3)
-    ca1(3)
-    cb2(3)
-    gi_a(2)
+    gw(0)
+    gp2(3)
+    gw(1)
+    gw(2)
+    ca2(3)
     gi2(1)
-    gp2(3)
-    gw(0)
     gi_b(3)
-    ca2(3)
+    gi_a(3)
+    gi_c(3)
     gi3(1)
-    gw(1)
     gi2(2)
-    gw(2)
-    gi_a(3)
-    gi3(2)
     gw(3)
     gw(4)
     gw(5)
     gi3(3)
+    gi3(2)
 
     for store in stores + gw_stores[-2:]:
         store.wait()
@@ -528,15 +549,15 @@
             pltpu.VMEM((CHUNKS, 2, ROWS, B_WIDE), BF16),
             pltpu.VMEM((CHUNKS, 2, ROWS, B_COLS), BF16),
             pltpu.VMEM((CHUNKS, 2, 8, ROWS, COLS), BF16),
-            pltpu.VMEM((256, WIDTH), F32),
+            pltpu.VMEM((2, 256, WIDTH), F32),
             pltpu.VMEM((CHUNKS, 2, 2, 4, ROWS, WIDTH), BF16),
             pltpu.VMEM((CHUNKS - 1, 3, 2, 2, ROWS, WIDTH), BF16),
             pltpu.VMEM((7, 2, ROWS, WIDTH), BF16),
             pltpu.VMEM((CHUNKS - 1, 2, 2, ROWS, WIDTH), BF16),
             pltpu.VMEM((CHUNKS - 1, 2, ROWS, WIDTH), BF16),
             pltpu.VMEM((2, WIDTH, GROUP), BF16),
-            pltpu.SemaphoreType.DMA((CHUNKS, SLOTS)),
-            pltpu.SemaphoreType.DMA((CHUNKS, SLOTS)),
+            pltpu.SemaphoreType.DMA((SLOTS,)),
+            pltpu.SemaphoreType.DMA((SLOTS,)),
             pltpu.SemaphoreType.DMA((9,)),
         ],
         compiler_params=pltpu.CompilerParams(
@@ -547,7 +568,10 @@
     )(inputs.reshape(2, CHUNKS, ROWS, WIDTH), weight, cotangent.reshape(CHUNKS, ROWS, COLS))
 
 
-def last_tokens(sum_hbm, x_hbm, g_hbm, o_hbm, total, x_t, grads, sem, out_sem):
+def last_tokens(
+    sum_hbm, x_hbm, g_hbm, act_hbm, gi_hbm, o_hbm, act_out, gi_out,
+    total, x_t, grads, act, gi, sem, out_sem,
+):
     groups = COLS // GROUP
     tokens = pltpu.make_async_copy(x_hbm, x_t, sem.at[0])
     tokens.start()
@@ -561,6 +585,12 @@
         for load in pair:
             load.start()
         loads.append(pair)
+    small = (
+        (pltpu.make_async_copy(act_hbm, act, sem.at[1 + 2 * groups]), act, act_out),
+        (pltpu.make_async_copy(gi_hbm, gi, sem.at[2 + 2 * groups]), gi, gi_out),
+    )
+    for load, _, _ in small:
+        load.start()
     tokens.wait()
     stores = []
     for g in range(groups):
@@ -579,34 +609,45 @@
         store = pltpu.make_async_copy(total.at[g], o_hbm.at[:, g * GROUP : (g + 1) * GROUP], out_sem.at[g])
         store.start()
         stores.append(store)
+    for n, (load, held, out) in enumerate(small):
+        load.wait()
+        store = pltpu.make_async_copy(held, out, out_sem.at[groups + n])
+        store.start()
+        stores.append(store)
     for store in stores:
         store.wait()
 
 
-def add_last(partial, tokens, grads):
+def add_last(partial, tokens, grads, activated, grad_input):
     hbm = pl.BlockSpec(memory_space=pl.ANY)
     groups = COLS // GROUP
     return pl.pallas_call(
         last_tokens,
-        out_shape=jax.ShapeDtypeStruct((WIDTH, COLS), BF16),
-        in_specs=[hbm, hbm, hbm],
-        out_specs=hbm,
+        out_shape=(
+            jax.ShapeDtypeStruct((WIDTH, COLS), BF16),
+            jax.ShapeDtypeStruct(activated.shape, BF16),
+            jax.ShapeDtypeStruct(grad_input.shape, BF16),
+        ),
+        in_specs=[hbm] * 5,
+        out_specs=(hbm, hbm, hbm),
         scratch_shapes=[
             pltpu.VMEM((groups, WIDTH, GROUP), BF16),
             pltpu.VMEM((WIDTH, 256), BF16),
             pltpu.VMEM((2, 8, ROWS, COLS), BF16),
-            pltpu.SemaphoreType.DMA((1 + 2 * groups,)),
-            pltpu.SemaphoreType.DMA((groups,)),
+            pltpu.VMEM(activated.shape, BF16),
+            pltpu.VMEM(grad_input.shape, BF16),
+            pltpu.SemaphoreType.DMA((3 + 2 * groups,)),
+            pltpu.SemaphoreType.DMA((groups + 2,)),
         ],
         compiler_params=pltpu.CompilerParams(vmem_limit_bytes=60 * 2**20),
         cost_estimate=pl.CostEstimate(flops=2 * 256 * WIDTH * COLS, bytes_accessed=24 * 2**20, transcendentals=0),
         name="add_last",
-    )(partial, tokens, grads)
+    )(partial, tokens, grads, activated, grad_input)
 
 
 def shards(inputs, weight, cotangent):
     activated, grad_input, partial, grads, tokens = exchange(inputs, weight, cotangent)
-    grad_weight = add_last(partial, tokens, grads)
+    grad_weight, activated, grad_input = add_last(partial, tokens, grads, activated, grad_input)
     return activated.reshape(64, COLS), grad_input.reshape(128, WIDTH), grad_weight
 
 

time: 142 us -> 137 us (0.965)
  Pallas kernels: 139 us -> 136 us
  local copies, waits for them, and re-layouts: 1.57 us -> 0 us
    pallas_call x1, Pallas kernels: 130 us -> 126 us  [exchange(): pl.pallas_call(kernel, out_shape=(jax.ShapeDtypeStruct((CHUNKS, ROWS, COL...]
    unnamed x6 -> x0, local copies, waits for them, and re-layouts: 1.57 us -> none
where the time goes in v3:
time: 137 us
  Pallas kernels  136 us (99%)
    pallas_call x1, Pallas kernels, exchange(): pl.pallas_call(kernel, out_shape=(jax.ShapeDtypeStruct((CHUNKS, ROWS, COL...  126 us
    pallas_call x1, Pallas kernels, add_last(): pl.pallas_call(last_tokens, out_shape=(jax.ShapeDtypeStruct((WIDTH, COLS)...  9.4 us

profile of v3, /device:TPU:1, one launch (start us, length us, event | category | flops | bytes accessed | tf_op | source)
XLA Modules:
  0.0 136.6 jit_solution(6320348299739541907)
XLA Ops:
  0.6 126.4 %exchange.1 = (bf16[4,16,6144]{2,1,0:T(8,128)(2,1)}, bf16[2,4,16,768]{3,2,1,0:T(8,128)(2,1)}, bf16[6,768,1024]{2,1,0:T(8,128)(2,1)}, bf16[2,8,16,6144]{3,2,1,0:T(8,128)(2,1)}, bf16[768,256]{1,0:T(8,128)(2,1)}) custom-call(bf16[2,4,16,768]{3,2,1,0:T(8,128)(2,1)} %bitcast.6, bf16[768,6144]{1,0:T(8,128)(2,1)} %w_hbm.1, bf16[4,16,6144]{2,1,0:T(8,128)(2,1)} %bitcast.4), custom_call_target="tpu_custom_call" | custom-call | flops 24159191040 | bytes 25165824 | tf_op jit(solution)/shard_map/exchange/pallas_call | solution.py:525
  127.1 9.4 %add_last.1 = (bf16[768,6144]{1,0:T(8,128)(2,1)}, bf16[4,16,6144]{2,1,0:T(8,128)(2,1)}, bf16[2,4,16,768]{3,2,1,0:T(8,128)(2,1)}) custom-call(bf16[6,768,1024]{2,1,0:T(8,128)(2,1)} %get-tuple-element.11.sum_hbm, bf16[768,256]{1,0:T(8,128)(2,1)} %get-tuple-element.12.x_hbm, bf16[2,8,16,6144]{3,2,1,0:T(8,128)(2,1)} %get-tuple-element.13.g_hbm, ...), custom_call_target="tpu_custom_call" | custom-call | flops 2415919104 | bytes 25165824 | tf_op jit(solution)/shard_map/add_last/pallas_call | solution.py:624

commit v4 on v3

--- a/solution.py
+++ b/solution.py
@@ -41,9 +41,9 @@
 
 
 def kernel(
-    x_ref, w_hbm, cot_ref,
-    act_ref, gi_ref, gw_hbm, g_out, x_out,
-    w, xs, xt, xt_last, part, share, ah, ra, ta, ay, rb, tb, bh, rbx, grad, acc, gi, rz, rd, ti, ry, stage,
+    x_hbm, w_hbm, cot_hbm,
+    act_out, gi_out, gw_hbm, g_out, x_out,
+    w, xs, xt, xt_last, part, share, ah, ra, ta, ay, rb, tb, bh, rbx, grad, acc, gi, rz, rd, ti, ry, stage, cot_ref, act_ref, gi_ref,
     send_sem, recv_sem, local_sem,
 ):
     row, col = lax.axis_index("row"), lax.axis_index("col")
@@ -65,8 +65,13 @@
     both_peer = {d: device(ylo=1 - ylo, z=z_at[d]) for d in HOPS}
     peers = [y_peer, core_peer, ylo_peer, *x_peer, *z_peer.values(), *both_peer.values()]
 
+    load_x = [
+        pltpu.make_async_copy(x_hbm.at[:, k], xs.at[k, :, col], local_sem.at[9 + k]) for k in range(CHUNKS)
+    ]
     load_w = pltpu.make_async_copy(w_hbm, w, local_sem.at[0])
-    load_w.start()
+    load_cot = pltpu.make_async_copy(cot_hbm, cot_ref, local_sem.at[13])
+    for load in (*load_x, load_w, load_cot):
+        load.start()
 
     barrier = pltpu.get_barrier_semaphore()
     for peer in peers:
@@ -107,13 +112,12 @@
         return share.at[k].reshape(2, 4, ROWS, COLS)
 
     def x_start(k):
-        xs[k, :, col] = x_ref[:, k]
-        send(k, "xy", x_ref.at[:, k], xs.at[k, :, col], ylo_peer)
+        send(k, "xy", x_hbm.at[:, k], xs.at[k, :, col], ylo_peer)
         for d in (1, 3, 2):
-            send(k, ("xz", d), x_ref.at[:, k], xs.at[k, :, col], z_peer[d])
+            send(k, ("xz", d), x_hbm.at[:, k], xs.at[k, :, col], z_peer[d])
         if k == 0:
             for d in (1, 3, 2):
-                send(k, ("xf", d), x_ref.at[:, k], xs.at[k, :, col], both_peer[d])
+                send(k, ("xf", d), x_hbm.at[:, k], xs.at[k, :, col], both_peer[d])
 
     def x_forward(k):
         arrived(k, "xy")
@@ -134,6 +138,7 @@
             load_w.wait()
         if k not in waited:
             waited.add(k)
+            load_x[k].wait()
             arrived(k, *(["xy"] if k == 0 else []), *each("xz", HOPS), *each("xf", HOPS))
         if k >= 2:
             sent(k - 2, name)
@@ -217,13 +222,28 @@
     def pass_on(k, name, ref, peer):
         send(k, name, ref, ref, peer)
 
+    activated = []
+
+    def before_activate():
+        if not activated:
+            load_cot.wait()
+
+    def after_activate(k):
+        activated.append(k)
+        if activated.count(k) == 2:
+            store = pltpu.make_async_copy(act_ref.at[k], act_out.at[k], local_sem.at[14 + k])
+            store.start()
+            stores.append(store)
+
     def fin_a(k):
         arrived(k, "ay")
+        before_activate()
 
         def body(tile):
             activate(k, ta[k, yhi, :, tile].astype(F32) + ay[k, :, tile].astype(F32), tile)
 
         tiles(0, A_COLS, body)
+        after_activate(k)
         mine = block(k, yhi, x, A)
         pass_on(k, "gAy", mine, y_peer)
         for h in WAYS:
@@ -231,6 +251,7 @@
 
     def fin_b(k):
         arrived(k, *each("bn", WAYS), *each("bm", WAYS))
+        before_activate()
 
         @pl.loop(0, B_COLS // TILE)
         def _(j):
@@ -238,6 +259,7 @@
             pre = tb[k, x, :, here].astype(F32) + rbx[k, 0, :, here].astype(F32) + rbx[k, 1, :, here].astype(F32)
             activate(k, pre, pl.ds(pl.multiple_of(A_COLS + j * TILE, TILE), TILE))
 
+        after_activate(k)
         mine = block(k, yhi, x, B)
         for h in WAYS:
             pass_on(k, ("gB", h), mine, x_peer[h])
@@ -360,6 +382,9 @@
             for d in range(7):
                 total += rd[d].astype(F32)
         gi_ref[:, k] = total.astype(BF16)
+        store = pltpu.make_async_copy(gi_ref.at[:, k], gi_out.at[:, k], local_sem.at[18 + k])
+        store.start()
+        stores.append(store)
 
     def gw(g):
         slot = g % 2
@@ -520,7 +545,6 @@
 
 
 def exchange(inputs, weight, cotangent):
-    vmem = pl.BlockSpec(memory_space=pltpu.VMEM)
     hbm = pl.BlockSpec(memory_space=pl.ANY)
     return pl.pallas_call(
         kernel,
@@ -531,8 +555,8 @@
             jax.ShapeDtypeStruct((2, 8, ROWS, COLS), BF16),
             jax.ShapeDtypeStruct((WIDTH, 256), BF16),
         ),
-        in_specs=[vmem, hbm, vmem],
-        out_specs=(vmem, vmem, hbm, hbm, hbm),
+        in_specs=[hbm] * 3,
+        out_specs=(hbm,) * 5,
         scratch_shapes=[
             pltpu.VMEM((WIDTH, COLS), BF16),
             pltpu.VMEM((CHUNKS, 2, 8, ROWS, WIDTH), BF16),
@@ -556,9 +580,12 @@
             pltpu.VMEM((CHUNKS - 1, 2, 2, ROWS, WIDTH), BF16),
             pltpu.VMEM((CHUNKS - 1, 2, ROWS, WIDTH), BF16),
             pltpu.VMEM((2, WIDTH, GROUP), BF16),
+            pltpu.VMEM((CHUNKS, ROWS, COLS), BF16),
+            pltpu.VMEM((CHUNKS, ROWS, COLS), BF16),
+            pltpu.VMEM((2, CHUNKS, ROWS, WIDTH), BF16),
             pltpu.SemaphoreType.DMA((SLOTS,)),
             pltpu.SemaphoreType.DMA((SLOTS,)),
-            pltpu.SemaphoreType.DMA((9,)),
+            pltpu.SemaphoreType.DMA((22,)),
         ],
         compiler_params=pltpu.CompilerParams(
             collective_id=0, has_side_effects=True, vmem_limit_bytes=61 * 2**20

time: 137 us -> 135 us (0.985)
  Pallas kernels: 136 us -> 134 us
    pallas_call x1, Pallas kernels: 126 us -> 125 us  [exchange(): pl.pallas_call(kernel, out_shape=(jax.ShapeDtypeStruct((CHUNKS, ROWS, COL...]
where the time goes in v4:
time: 135 us
  Pallas kernels  134 us (99%)
    pallas_call x1, Pallas kernels, exchange(): pl.pallas_call(kernel, out_shape=(jax.ShapeDtypeStruct((CHUNKS, ROWS, COL...  125 us
    pallas_call x1, Pallas kernels, add_last(): pl.pallas_call(last_tokens, out_shape=(jax.ShapeDtypeStruct((WIDTH, COLS)...  9.4 us

profile of v4, /device:TPU:1, one launch (start us, length us, event | category | flops | bytes accessed | tf_op | source)
XLA Modules:
  0.0 134.8 jit_solution(14120447535752230921)
XLA Ops:
  0.6 124.7 %exchange.1 = (bf16[4,16,6144]{2,1,0:T(8,128)(2,1)}, bf16[2,4,16,768]{3,2,1,0:T(8,128)(2,1)}, bf16[6,768,1024]{2,1,0:T(8,128)(2,1)}, bf16[2,8,16,6144]{3,2,1,0:T(8,128)(2,1)}, bf16[768,256]{1,0:T(8,128)(2,1)}) custom-call(bf16[2,4,16,768]{3,2,1,0:T(8,128)(2,1)} %bitcast.6, bf16[768,6144]{1,0:T(8,128)(2,1)} %w_hbm.1, bf16[4,16,6144]{2,1,0:T(8,128)(2,1)} %bitcast.4), custom_call_target="tpu_custom_call" | custom-call | flops 24159191040 | bytes 25165824 | tf_op jit(solution)/shard_map/exchange/pallas_call | solution.py:549
  125.3 9.4 %add_last.1 = (bf16[768,6144]{1,0:T(8,128)(2,1)}, bf16[4,16,6144]{2,1,0:T(8,128)(2,1)}, bf16[2,4,16,768]{3,2,1,0:T(8,128)(2,1)}) custom-call(bf16[6,768,1024]{2,1,0:T(8,128)(2,1)} %get-tuple-element.11.sum_hbm, bf16[768,256]{1,0:T(8,128)(2,1)} %get-tuple-element.12.x_hbm, bf16[2,8,16,6144]{3,2,1,0:T(8,128)(2,1)} %get-tuple-element.13.g_hbm, ...), custom_call_target="tpu_custom_call" | custom-call | flops 2415919104 | bytes 25165824 | tf_op jit(solution)/shard_map/add_last/pallas_call | solution.py:651

commit v5 on v4

--- a/solution.py
+++ b/solution.py
@@ -407,6 +407,10 @@
         )
         store.start()
         gw_stores.append(store)
+
+    def drain():
+        for copy in unsent.values():
+            copy.wait_send()
 
     x_start(0)
     x_start(1)
@@ -524,24 +528,23 @@
     gw(0)
     gp2(3)
     gw(1)
-    gw(2)
     ca2(3)
     gi2(1)
     gi_b(3)
     gi_a(3)
     gi_c(3)
+    gw(2)
     gi3(1)
     gi2(2)
     gw(3)
     gw(4)
     gw(5)
+    gi3(2)
+    drain()
     gi3(3)
-    gi3(2)
 
     for store in stores + gw_stores[-2:]:
         store.wait()
-    for copy in unsent.values():
-        copy.wait_send()
 
 
 def exchange(inputs, weight, cotangent):

time: 135 us -> 136 us (level)
  no operation moved by 1% of the time
where the time goes in v5:
time: 136 us
  Pallas kernels  135 us (99%)
    pallas_call x1, Pallas kernels, exchange(): pl.pallas_call(kernel, out_shape=(jax.ShapeDtypeStruct((CHUNKS, ROWS, COL...  126 us
    pallas_call x1, Pallas kernels, add_last(): pl.pallas_call(last_tokens, out_shape=(jax.ShapeDtypeStruct((WIDTH, COLS)...  9.4 us

profile of v5, /device:TPU:1, one launch (start us, length us, event | category | flops | bytes accessed | tf_op | source)
XLA Modules:
  0.0 136.1 jit_solution(18280433986976629349)
XLA Ops:
  0.6 125.9 %exchange.1 = (bf16[4,16,6144]{2,1,0:T(8,128)(2,1)}, bf16[2,4,16,768]{3,2,1,0:T(8,128)(2,1)}, bf16[6,768,1024]{2,1,0:T(8,128)(2,1)}, bf16[2,8,16,6144]{3,2,1,0:T(8,128)(2,1)}, bf16[768,256]{1,0:T(8,128)(2,1)}) custom-call(bf16[2,4,16,768]{3,2,1,0:T(8,128)(2,1)} %bitcast.6, bf16[768,6144]{1,0:T(8,128)(2,1)} %w_hbm.1, bf16[4,16,6144]{2,1,0:T(8,128)(2,1)} %bitcast.4), custom_call_target="tpu_custom_call" | custom-call | flops 24159191040 | bytes 25165824 | tf_op jit(solution)/shard_map/exchange/pallas_call | solution.py:552
  126.5 9.4 %add_last.1 = (bf16[768,6144]{1,0:T(8,128)(2,1)}, bf16[4,16,6144]{2,1,0:T(8,128)(2,1)}, bf16[2,4,16,768]{3,2,1,0:T(8,128)(2,1)}) custom-call(bf16[6,768,1024]{2,1,0:T(8,128)(2,1)} %get-tuple-element.11.sum_hbm, bf16[768,256]{1,0:T(8,128)(2,1)} %get-tuple-element.12.x_hbm, bf16[2,8,16,6144]{3,2,1,0:T(8,128)(2,1)} %get-tuple-element.13.g_hbm, ...), custom_call_target="tpu_custom_call" | custom-call | flops 2415919104 | bytes 25165824 | tf_op jit(solution)/shard_map/add_last/pallas_call | solution.py:654

commit v6 on v5

--- a/solution.py
+++ b/solution.py
@@ -528,12 +528,12 @@
     gw(0)
     gp2(3)
     gw(1)
+    gw(2)
     ca2(3)
     gi2(1)
     gi_b(3)
     gi_a(3)
     gi_c(3)
-    gw(2)
     gi3(1)
     gi2(2)
     gw(3)

time: 136 us -> 135 us (level)
    pallas_call x1, Pallas kernels: 126 us -> 124 us  [exchange(): pl.pallas_call(kernel, out_shape=(jax.ShapeDtypeStruct((CHUNKS, ROWS, COL...]
where the time goes in v6:
time: 135 us
  Pallas kernels  134 us (99%)
    pallas_call x1, Pallas kernels, exchange(): pl.pallas_call(kernel, out_shape=(jax.ShapeDtypeStruct((CHUNKS, ROWS, COL...  124 us
    pallas_call x1, Pallas kernels, add_last(): pl.pallas_call(last_tokens, out_shape=(jax.ShapeDtypeStruct((WIDTH, COLS)...  9.4 us

profile of v6, /device:TPU:1, one launch (start us, length us, event | category | flops | bytes accessed | tf_op | source)
XLA Modules:
  0.0 134.5 jit_solution(1080211969894161001)
XLA Ops:
  0.6 124.3 %exchange.1 = (bf16[4,16,6144]{2,1,0:T(8,128)(2,1)}, bf16[2,4,16,768]{3,2,1,0:T(8,128)(2,1)}, bf16[6,768,1024]{2,1,0:T(8,128)(2,1)}, bf16[2,8,16,6144]{3,2,1,0:T(8,128)(2,1)}, bf16[768,256]{1,0:T(8,128)(2,1)}) custom-call(bf16[2,4,16,768]{3,2,1,0:T(8,128)(2,1)} %bitcast.6, bf16[768,6144]{1,0:T(8,128)(2,1)} %w_hbm.1, bf16[4,16,6144]{2,1,0:T(8,128)(2,1)} %bitcast.4), custom_call_target="tpu_custom_call" | custom-call | flops 24159191040 | bytes 25165824 | tf_op jit(solution)/shard_map/exchange/pallas_call | solution.py:552
  125.0 9.4 %add_last.1 = (bf16[768,6144]{1,0:T(8,128)(2,1)}, bf16[4,16,6144]{2,1,0:T(8,128)(2,1)}, bf16[2,4,16,768]{3,2,1,0:T(8,128)(2,1)}) custom-call(bf16[6,768,1024]{2,1,0:T(8,128)(2,1)} %get-tuple-element.11.sum_hbm, bf16[768,256]{1,0:T(8,128)(2,1)} %get-tuple-element.12.x_hbm, bf16[2,8,16,6144]{3,2,1,0:T(8,128)(2,1)} %get-tuple-element.13.g_hbm, ...), custom_call_target="tpu_custom_call" | custom-call | flops 2415919104 | bytes 25165824 | tf_op jit(solution)/shard_map/add_last/pallas_call | solution.py:654
